TPU v7x, 32 devices: a whole 2x2x4 slice. The times are simulated.
32 devices in a mesh: seq: 8 (over z, y), ch: 4 (over x, core).
Axes of the slice: x: 2, y: 2, z: 4, core: 2. Of those that a mesh axis runs over, the one named last changes fastest.
Arguments:
- tokens: bfloat16 [1024, 2048], P('seq'), may hold values from -6 to 6
- in_weight: bfloat16 [2048, 3, 2048], P('seq', None, 'ch'), may hold values from -0.125 to 0.125
- filter_taps: float32 [1024, 2048], P('seq', 'ch'), may hold values from -1.1 to 1.1
- skip_gain: float32 [2048], P('ch'), may hold values from 0.5 to 1.5
- out_weight: bfloat16 [2048, 2048], P(None, 'ch'), may hold values from -0.125 to 0.125
Outputs:
- mixed: bfloat16 [1024, 2048], P('seq', 'ch')
All inputs are finite; a program needn't handle non-finite values.
Results may differ from a plain program's by a relative error of at most 0.0072.
Values may be sent and summed in bfloat16 or wider, within the bound.
A program may use at most 64 MiB of HBM per device.

v0:
```python
import math

import jax
import jax.numpy as jnp
from jax import lax
from jax.sharding import PartitionSpec as P

HIGHEST_PREC = lax.Precision.HIGHEST


def angle_table(first_index, second_index, period):
    product = first_index[:, None] * second_index[None, :] % period
    angle = 2.0 * math.pi / period * product.astype(jnp.float32)
    return (jnp.cos(angle), jnp.sin(angle))


def contract(matrix, blocks):
    return jnp.einsum("kn,...nc->...kc", matrix, blocks, precision=HIGHEST_PREC)


def rotate(real_part, imag_part, cosine, sine, direction):
    return (
        real_part * cosine - direction * imag_part * sine,
        imag_part * cosine + direction * real_part * sine,
    )


def spectral(parts):
    sig_re, sig_im, filt_re, filt_im = parts
    row_count = sig_re.shape[-2]
    index = jnp.arange(row_count, dtype=jnp.int32)
    cosine, sine = angle_table(index, index, row_count)

    def forward(real_part, imag_part):
        return (
            contract(cosine, real_part) + contract(sine, imag_part),
            contract(cosine, imag_part) - contract(sine, real_part),
        )

    spec_re, spec_im = forward(sig_re, sig_im)
    resp_re, resp_im = forward(filt_re, filt_im)
    prod_re = spec_re * resp_re - spec_im * resp_im
    prod_im = spec_re * resp_im + spec_im * resp_re
    return (
        contract(cosine, prod_re) - contract(sine, prod_im),
        contract(cosine, prod_im) + contract(sine, prod_re),
    )


def per_device(tokens, in_weight, filter_taps, skip_gain, out_weight):
    row_count, channel_count = filter_taps.shape
    seq_size = lax.axis_size("seq")
    seq_index = lax.axis_index("seq")
    full_len = 2 * seq_size * row_count
    radix = 2 * seq_size
    positions = jnp.arange(row_count, dtype=jnp.int32)
    piece = lax.all_gather(in_weight, "seq", axis=0, tiled=True)
    width_rows = piece.shape[0]
    projected = jnp.dot(
        tokens, piece.reshape(width_rows, 3 * channel_count), preferred_element_type=jnp.float32
    )
    projected = projected.astype(jnp.bfloat16).reshape(row_count, 3, channel_count)
    values = projected[:, 0].astype(jnp.float32)
    in_gate = projected[:, 1].astype(jnp.float32)
    out_gate = projected[:, 2].astype(jnp.float32)
    signal = in_gate * values
    block_rows = row_count // seq_size
    sig_cols, filt_cols = (
        lax.all_to_all(
            signal.reshape(1, row_count, channel_count),
            "seq",
            split_axis=1,
            concat_axis=0,
            tiled=True,
        ),
        lax.all_to_all(
            filter_taps.reshape(1, row_count, channel_count),
            "seq",
            split_axis=1,
            concat_axis=0,
            tiled=True,
        ),
    )
    first_cos, first_sin = angle_table(
        jnp.arange(radix, dtype=jnp.int32), jnp.arange(seq_size, dtype=jnp.int32), radix
    )
    offsets = seq_index * block_rows + jnp.arange(block_rows, dtype=jnp.int32)
    turn_cos, turn_sin = angle_table(jnp.arange(radix, dtype=jnp.int32), offsets, full_len)
    sectioned = []
    for column_data in (sig_cols, filt_cols):
        part_re = jnp.einsum("kp,pqc->kqc", first_cos, column_data, precision=HIGHEST_PREC)
        part_im = -jnp.einsum("kp,pqc->kqc", first_sin, column_data, precision=HIGHEST_PREC)
        turned_re, turned_im = rotate(
            part_re, part_im, turn_cos[:, :, None], turn_sin[:, :, None], -1.0
        )
        sectioned.append(turned_re.reshape(seq_size, 2, block_rows, channel_count))
        sectioned.append(turned_im.reshape(seq_size, 2, block_rows, channel_count))
    back_re, back_im = spectral(
        (
            lax.all_to_all(sectioned[0], "seq", split_axis=0, concat_axis=2, tiled=True),
            lax.all_to_all(sectioned[1], "seq", split_axis=0, concat_axis=2, tiled=True),
            lax.all_to_all(sectioned[2], "seq", split_axis=0, concat_axis=2, tiled=True),
            lax.all_to_all(sectioned[3], "seq", split_axis=0, concat_axis=2, tiled=True),
        )
    )
    own_freq = 2 * seq_index + jnp.arange(2, dtype=jnp.int32)
    inv_cos, inv_sin = angle_table(own_freq, positions, full_len)
    inner_re, inner_im = rotate(
        back_re[0], back_im[0], inv_cos[:, :, None], inv_sin[:, :, None], 1.0
    )
    gathered_re, gathered_im = (
        lax.all_to_all(inner_re, "seq", split_axis=1, concat_axis=0, tiled=True),
        lax.all_to_all(inner_im, "seq", split_axis=1, concat_axis=0, tiled=True),
    )
    last_cos, last_sin = angle_table(
        jnp.arange(seq_size, dtype=jnp.int32), jnp.arange(radix, dtype=jnp.int32), radix
    )
    rows_part = (
        jnp.einsum("pk,kqc->pqc", last_cos, gathered_re, precision=HIGHEST_PREC)
        - jnp.einsum("pk,kqc->pqc", last_sin, gathered_im, precision=HIGHEST_PREC)
    ) / full_len
    conv = lax.all_to_all(rows_part, "seq", split_axis=0, concat_axis=1, tiled=True).reshape(
        row_count, channel_count
    )
    gated = (out_gate * (conv + skip_gain[None, :] * signal)).astype(jnp.bfloat16)
    whole = lax.all_gather(gated, "ch", axis=1, tiled=True)
    return jnp.dot(whole, out_weight, preferred_element_type=jnp.float32).astype(jnp.bfloat16)


def solution(mesh):
    in_specs = (P("seq", None), P("seq", None, "ch"), P("seq", "ch"), P("ch"), P(None, "ch"))
    out_specs = P("seq", "ch")
    return jax.shard_map(
        per_device, mesh=mesh, in_specs=in_specs, out_specs=out_specs, check_vma=False
    )
```

profile of v0, /device:TPU:0, one launch (start us, length us, event | category | flops | bytes accessed | tf_op | source)
XLA Modules:
  0.0 286.5 jit_solution(9593525473594588162)
XLA Ops:
  6.5 2.5 copy.38
  9.0 1.8 reshape.241
  10.8 7.3 %all-to-all-start.3 = ((f32[1,128,512]{2,0,1:T(1,128)}), f32[1,128,512]{2,0,1:T(1,128)S(1)}, u32[]{:S(2)}, u32[]{:S(2)}) async-start(f32[1,128,512]{2,0,1:T(1,128)} %reshape.241), calls=%async_computation.3 | async-start | bytes 524288 | tf_op jit(solution)/shard_map/all_to_all | solution.py:76
  18.1 95.6 %all-gather.2.cloned.1.call-done = bf16[2048,3,512]{0,2,1:T(8,128)(2,1)} async-done(((bf16[256,3,512]{0,2,1:T(8,128)(2,1)}), bf16[2048,3,512]{0,2,1:T(8,128)(2,1)}) %all-gather.2.cloned.1.call-update) | async-done | bytes 6291472 | tf_op jit(solution)/shard_map/all_gather | solution.py:57
  113.7 5.2 %convolution_convert_fusion = bf16[128,1536]{1,0:T(8,128)(2,1)S(1)} fusion(bf16[128,2048]{1,0:T(8,128)(2,1)} %param.5, bf16[2048,1536]{0,1:T(8,128)(2,1)} %bitcast.146), kind=kOutput, calls=%fused_computation | convolution fusion | flops 805502976 | bytes 7208960 | tf_op jit(solution)/shard_map/dot_general | solution.py:59
  120.0 3.4 %all-to-all-start = ((f32[1,128,512]{2,0,1:T(1,128)}), f32[1,128,512]{2,0,1:T(1,128)S(1)}, u32[]{:S(2)}, u32[]{:S(2)}) async-start(f32[1,128,512]{2,0,1:T(1,128)} %copy.40), calls=%async_computation | async-start | bytes 524288 | tf_op jit(solution)/shard_map/all_to_all | solution.py:69
  125.1 7.0 %all-to-all-done = f32[1,128,512]{2,0,1:T(1,128)S(1)} async-done(((f32[1,128,512]{2,0,1:T(1,128)}), f32[1,128,512]{2,0,1:T(1,128)S(1)}, u32[]{:S(2)}, u32[]{:S(2)}) %all-to-all-start) | async-done | bytes 262176 | tf_op jit(solution)/shard_map/all_to_all | solution.py:69
  133.5 2.9 %multiply_add_fusion.2 = (f32[16,16,512]{2,0,1:T(8,128)}, f32[16,16,512]{2,0,1:T(8,128)S(1)}, f32[16,16,512]{2,0,1:T(8,128)S(1)}, f32[16,16,512]{2,0,1:T(8,128)}) fusion(f32[16,16,512]{2,0,1:T(8,128)} %convolution_negate_fusion, f32[16,16]{0,1:T(8,128)S(1)} %get-tuple-element.18, f32[16,16]{0,1:T(8,128)S(1)} %get-tuple-element.17, ...), kind=kOutput, calls=%fused_computation.24 | convolution fusion | flops 14157568 | bytes 3934208 | tf_op jit(solution)/shard_map/kp,pqc->kqc/dot_general | solution.py:91
  137.5 3.6 %all-to-all-start.4 = ((f32[8,2,16,512]{3,2,1,0:T(8,128)}), f32[8,2,16,512]{3,2,1,0:T(8,128)S(1)}, u32[]{:S(2)}, u32[]{:S(2)}) async-start(f32[8,2,16,512]{3,2,1,0:T(8,128)} %bitcast.164), calls=%async_computation.4 | async-start | bytes 1048576 | tf_op jit(solution)/shard_map/all_to_all | solution.py:102
  141.1 2.1 copy.80
  143.2 11.9 %all-to-all-done.4 = f32[8,2,16,512]{3,2,1,0:T(8,128)S(1)} async-done(((f32[8,2,16,512]{3,2,1,0:T(8,128)}), f32[8,2,16,512]{3,2,1,0:T(8,128)S(1)}, u32[]{:S(2)}, u32[]{:S(2)}) %all-to-all-start.4) | async-done | bytes 524320 | tf_op jit(solution)/shard_map/all_to_all | solution.py:102
  155.1 4.1 %all-to-all-start.5 = ((f32[8,2,16,512]{3,2,1,0:T(8,128)}), f32[8,2,16,512]{3,2,1,0:T(8,128)}, u32[]{:S(2)}, u32[]{:S(2)}) async-start(f32[8,2,16,512]{3,2,1,0:T(8,128)} %bitcast.163), calls=%async_computation.5 | async-start | bytes 1048576 | tf_op jit(solution)/shard_map/all_to_all | solution.py:103
  159.3 2.1 copy.77
  161.4 11.7 %all-to-all-done.5 = f32[8,2,16,512]{3,2,1,0:T(8,128)} async-done(((f32[8,2,16,512]{3,2,1,0:T(8,128)}), f32[8,2,16,512]{3,2,1,0:T(8,128)}, u32[]{:S(2)}, u32[]{:S(2)}) %all-to-all-start.5) | async-done | bytes 524320 | tf_op jit(solution)/shard_map/all_to_all | solution.py:103
  173.1 4.1 %all-to-all-start.1 = ((f32[8,2,16,512]{3,2,1,0:T(8,128)}), f32[8,2,16,512]{3,2,1,0:T(8,128)}, u32[]{:S(2)}, u32[]{:S(2)}) async-start(f32[8,2,16,512]{3,2,1,0:T(8,128)} %bitcast.161), calls=%async_computation.1 | async-start | bytes 1048576 | tf_op jit(solution)/shard_map/all_to_all | solution.py:100
  178.6 1.9 copy.55
  180.5 10.5 %all-to-all-done.1 = f32[8,2,16,512]{3,2,1,0:T(8,128)} async-done(((f32[8,2,16,512]{3,2,1,0:T(8,128)}), f32[8,2,16,512]{3,2,1,0:T(8,128)}, u32[]{:S(2)}, u32[]{:S(2)}) %all-to-all-start.1) | async-done | bytes 524320 | tf_op jit(solution)/shard_map/all_to_all | solution.py:100
  191.0 4.3 %all-to-all-start.2 = ((f32[8,2,16,512]{3,2,1,0:T(8,128)}), f32[8,2,16,512]{3,2,1,0:T(8,128)}, u32[]{:S(2)}, u32[]{:S(2)}) async-start(f32[8,2,16,512]{3,2,1,0:T(8,128)} %bitcast.162), calls=%async_computation.2 | async-start | bytes 1048576 | tf_op jit(solution)/shard_map/all_to_all | solution.py:101
  197.5 1.9 fusion.35
  199.4 3.0 %fusion.29 = f32[2,512,128]{2,1,0:T(8,128)} fusion(f32[2,128,512]{2,1,0:T(8,128)} %bitcast.151), kind=kOutput, calls=%fused_computation.55 | convolution fusion | flops 201555968 | bytes 1048576 | tf_op jit(solution)/shard_map/kn,...nc->...kc/dot_general | solution.py:18
  202.4 3.0 %convolution_add_fusion.1 = f32[2,512,128]{2,1,0:T(8,128)} fusion(f32[2,512,128]{2,1,0:T(8,128)S(1)} %fusion.33, f32[2,128,512]{2,1,0:T(8,128)} %bitcast.152), kind=kOutput, calls=%fused_computation.9 | convolution fusion | flops 201687040 | bytes 1572864 | tf_op jit(solution)/shard_map/kn,...nc->...kc/dot_general | solution.py:18
  205.3 3.1 %all-to-all-done.2 = f32[8,2,16,512]{3,2,1,0:T(8,128)} async-done(((f32[8,2,16,512]{3,2,1,0:T(8,128)}), f32[8,2,16,512]{3,2,1,0:T(8,128)}, u32[]{:S(2)}, u32[]{:S(2)}) %all-to-all-start.2) | async-done | bytes 524320 | tf_op jit(solution)/shard_map/all_to_all | solution.py:101
  210.7 2.2 convolution_add_fusion.2
  212.8 2.2 convolution_subtract_fusion.1
  215.0 2.2 multiply_subtract_fusion.1
  221.8 3.8 %all-to-all-start.6 = ((f32[2,128,512]{2,0,1:T(2,128)}), f32[2,128,512]{2,0,1:T(2,128)S(1)}, u32[]{:S(2)}, u32[]{:S(2)}) async-start(f32[2,128,512]{2,0,1:T(2,128)} %copy.61), calls=%async_computation.6 | async-start | bytes 1048576 | tf_op jit(solution)/shard_map/all_to_all | solution.py:112
  226.6 12.8 %all-to-all-done.6 = f32[2,128,512]{2,0,1:T(2,128)S(1)} async-done(((f32[2,128,512]{2,0,1:T(2,128)}), f32[2,128,512]{2,0,1:T(2,128)S(1)}, u32[]{:S(2)}, u32[]{:S(2)}) %all-to-all-start.6) | async-done | bytes 524320 | tf_op jit(solution)/shard_map/all_to_all | solution.py:112
  239.4 3.6 %all-to-all-start.7 = ((f32[2,128,512]{2,0,1:T(2,128)}), f32[2,128,512]{2,0,1:T(2,128)S(1)}, u32[]{:S(2)}, u32[]{:S(2)}) async-start(f32[2,128,512]{2,0,1:T(2,128)} %copy.64), calls=%async_computation.7 | async-start | bytes 1048576 | tf_op jit(solution)/shard_map/all_to_all | solution.py:113
  244.7 2.1 fusion.71
  246.8 10.0 %all-to-all-done.7 = f32[2,128,512]{2,0,1:T(2,128)S(1)} async-done(((f32[2,128,512]{2,0,1:T(2,128)}), f32[2,128,512]{2,0,1:T(2,128)S(1)}, u32[]{:S(2)}, u32[]{:S(2)}) %all-to-all-start.7) | async-done | bytes 524320 | tf_op jit(solution)/shard_map/all_to_all | solution.py:113
  259.2 11.8 %all_to_all.129 = f32[8,16,512]{2,1,0:T(8,128)S(1)} all-to-all(f32[8,16,512]{2,1,0:T(8,128)S(1)} %copy.67), channel_id=1, replica_groups=mesh['seq'=8,'ch'=4] {'seq'}, dimensions={0} | all-to-all | bytes 524288 | tf_op jit(solution)/shard_map/all_to_all | solution.py:122
  271.2 7.3 %all_gather.7 = bf16[128,2048]{0,1:T(8,128)(2,1)S(1)} all-gather(bf16[128,512]{0,1:T(8,128)(2,1)S(1)} %fusion.9), channel_id=1, replica_groups=mesh['seq'=8,'ch'=4] {'ch'}, dimensions={1}, use_global_device_ids=true | all-gather | bytes 655360 | tf_op jit(solution)/shard_map/all_gather | solution.py:126
  (43 shorter events, 22.0 us)
Async XLA Ops:
  6.5 272.0 %copy-start = (bf16[2048,512]{1,0:T(8,128)(2,1)S(1)}, bf16[2048,512]{1,0:T(8,128)(2,1)}, u32[]{:S(2)}) copy-start(bf16[2048,512]{1,0:T(8,128)(2,1)} %param.9) | copy-start | bytes 6291460
  6.5 107.2 %all-gather.2.cloned.1.call-start = ((), (), s32[]{:S(2)}) async-start(), calls=%async_computation.9 | async-start | bytes 7077888 | tf_op jit(solution)/shard_map/all_gather | solution.py:57
  10.8 109.2 %all-to-all-start.3 = ((f32[1,128,512]{2,0,1:T(1,128)}), f32[1,128,512]{2,0,1:T(1,128)S(1)}, u32[]{:S(2)}, u32[]{:S(2)}) async-start(f32[1,128,512]{2,0,1:T(1,128)} %reshape.241), calls=%async_computation.3 | async-start | bytes 524288 | tf_op jit(solution)/shard_map/all_to_all | solution.py:76
  120.0 12.1 %all-to-all-start = ((f32[1,128,512]{2,0,1:T(1,128)}), f32[1,128,512]{2,0,1:T(1,128)S(1)}, u32[]{:S(2)}, u32[]{:S(2)}) async-start(f32[1,128,512]{2,0,1:T(1,128)} %copy.40), calls=%async_computation | async-start | bytes 524288 | tf_op jit(solution)/shard_map/all_to_all | solution.py:69
  137.5 17.6 %all-to-all-start.4 = ((f32[8,2,16,512]{3,2,1,0:T(8,128)}), f32[8,2,16,512]{3,2,1,0:T(8,128)S(1)}, u32[]{:S(2)}, u32[]{:S(2)}) async-start(f32[8,2,16,512]{3,2,1,0:T(8,128)} %bitcast.164), calls=%async_computation.4 | async-start | bytes 1048576 | tf_op jit(solution)/shard_map/all_to_all | solution.py:102
  155.1 18.0 %all-to-all-start.5 = ((f32[8,2,16,512]{3,2,1,0:T(8,128)}), f32[8,2,16,512]{3,2,1,0:T(8,128)}, u32[]{:S(2)}, u32[]{:S(2)}) async-start(f32[8,2,16,512]{3,2,1,0:T(8,128)} %bitcast.163), calls=%async_computation.5 | async-start | bytes 1048576 | tf_op jit(solution)/shard_map/all_to_all | solution.py:103
  173.1 17.9 %all-to-all-start.1 = ((f32[8,2,16,512]{3,2,1,0:T(8,128)}), f32[8,2,16,512]{3,2,1,0:T(8,128)}, u32[]{:S(2)}, u32[]{:S(2)}) async-start(f32[8,2,16,512]{3,2,1,0:T(8,128)} %bitcast.161), calls=%async_computation.1 | async-start | bytes 1048576 | tf_op jit(solution)/shard_map/all_to_all | solution.py:100
  191.0 17.5 %all-to-all-start.2 = ((f32[8,2,16,512]{3,2,1,0:T(8,128)}), f32[8,2,16,512]{3,2,1,0:T(8,128)}, u32[]{:S(2)}, u32[]{:S(2)}) async-start(f32[8,2,16,512]{3,2,1,0:T(8,128)} %bitcast.162), calls=%async_computation.2 | async-start | bytes 1048576 | tf_op jit(solution)/shard_map/all_to_all | solution.py:101
  221.8 49.3 %copy-start.1 = (f32[512]{0:T(512)S(1)}, f32[512]{0:T(512)}, u32[]{:S(2)}) copy-start(f32[512]{0:T(512)} %param.8) | copy-start | bytes 6148
  221.8 17.6 %all-to-all-start.6 = ((f32[2,128,512]{2,0,1:T(2,128)}), f32[2,128,512]{2,0,1:T(2,128)S(1)}, u32[]{:S(2)}, u32[]{:S(2)}) async-start(f32[2,128,512]{2,0,1:T(2,128)} %copy.61), calls=%async_computation.6 | async-start | bytes 1048576 | tf_op jit(solution)/shard_map/all_to_all | solution.py:112
  239.4 17.4 %all-to-all-start.7 = ((f32[2,128,512]{2,0,1:T(2,128)}), f32[2,128,512]{2,0,1:T(2,128)S(1)}, u32[]{:S(2)}, u32[]{:S(2)}) async-start(f32[2,128,512]{2,0,1:T(2,128)} %copy.64), calls=%async_computation.7 | async-start | bytes 1048576 | tf_op jit(solution)/shard_map/all_to_all | solution.py:113
Sparse Core Ops, SparseCore 0:
  9.4 104.2 all-gather.1
where the time goes:
time: 288 us; the launch traced here: 287 us
  waiting for transfers between devices  163 us (57%)
  matrix products  35.7 us (12%)
  starting transfers between devices  34.3 us (12%)
  local copies, waits for them, and re-layouts  20.8 us (7%)
  blocking collectives  19.1 us (7%)
  between operations  13.7 us (5%)
    all_gather x1, waiting for transfers between devices, per_device(): piece = lax.all_gather(in_weight, 'seq', axis=0, tiled=True)  95.6 us
    dot_general x12, matrix products, contract(): return jnp.einsum('kn,...nc->...kc', matrix, blocks, precision=HIGHEST_PREC)  20.1 us
    all_to_all x1, waiting for transfers between devices, per_device(): lax.all_to_all(inner_re, 'seq', split_axis=1, concat_axis=0, tiled=True)  12.8 us
    all_to_all x1, waiting for transfers between devices, per_device(): lax.all_to_all(sectioned[2], 'seq', split_axis=0, concat_axis=2, tiled=True)  11.9 us
    all_to_all x1, blocking collectives, per_device(): lax.all_to_all(rows_part, 'seq', split_axis=0, concat_axis=1, tiled=True)  11.8 us
    all_to_all x1, waiting for transfers between devices, per_device(): lax.all_to_all(sectioned[3], 'seq', split_axis=0, concat_axis=2, tiled=True)  11.7 us
    all_to_all x1, waiting for transfers between devices, per_device(): lax.all_to_all(sectioned[0], 'seq', split_axis=0, concat_axis=2, tiled=True)  10.5 us
    all_to_all x1, waiting for transfers between devices, per_device(): lax.all_to_all(inner_im, 'seq', split_axis=1, concat_axis=0, tiled=True)  9.96 us
  transfers between devices with their start and end apart: 9, of which 8 were waited for; matrix products, arithmetic and copies ran while one was open for 11% of the time, Pallas kernels for 0%

commit v1 on v0

--- a/solution.py
+++ b/solution.py
@@ -2,6 +2,7 @@
 
 import jax
 import jax.numpy as jnp
+import numpy as np
 from jax import lax
 from jax.sharding import PartitionSpec as P
 
@@ -47,7 +48,7 @@
     )
 
 
-def per_device(tokens, in_weight, filter_taps, skip_gain, out_weight):
+def per_device_long(tokens, in_weight, filter_taps, skip_gain, out_weight):
     row_count, channel_count = filter_taps.shape
     seq_size = lax.axis_size("seq")
     seq_index = lax.axis_index("seq")
@@ -127,9 +128,67 @@
     return jnp.dot(whole, out_weight, preferred_element_type=jnp.float32).astype(jnp.bfloat16)
 
 
+DENSE_LIMIT = 2048
+
+
+def half_step_tables(total):
+    index = np.arange(total, dtype=np.int64)
+    product = (2 * index[:, None] + 1) * index[None, :] % (4 * total)
+    angle = 2.0 * np.pi / (4 * total) * product
+    return np.cos(angle), np.sin(angle)
+
+
+def dot32(left, right):
+    return jnp.dot(left.astype(jnp.bfloat16), right.astype(jnp.bfloat16), preferred_element_type=jnp.float32)
+
+
+def per_device(tokens, in_weight, filter_taps, skip_gain, out_weight):
+    row_count, channel_count = filter_taps.shape
+    seq_size = lax.axis_size("seq")
+    seq_index = lax.axis_index("seq")
+    own = channel_count // seq_size
+    total = row_count * seq_size
+    cos_table, sin_table = half_step_tables(total)
+    table = jnp.asarray(np.concatenate([cos_table, sin_table]), jnp.bfloat16)
+    back = jnp.asarray(np.concatenate([cos_table.T, -sin_table.T], axis=1) / total, jnp.bfloat16)
+    all_tokens = lax.all_gather(tokens, "seq", axis=0, tiled=True)
+    weight = lax.all_to_all(
+        in_weight.reshape(-1, 3, seq_size, own).transpose(2, 0, 1, 3).reshape(seq_size, -1, 128),
+        "seq", split_axis=0, concat_axis=0, tiled=True,
+    ).reshape(all_tokens.shape[1], 3 * own)
+    taps = lax.all_to_all(
+        filter_taps.astype(jnp.bfloat16).reshape(row_count, seq_size, own).transpose(1, 0, 2).reshape(seq_size, -1, 128),
+        "seq", split_axis=0, concat_axis=0, tiled=True,
+    ).reshape(total, own)
+    gain = lax.dynamic_slice_in_dim(skip_gain, seq_index * own, own)
+    projected = jnp.dot(all_tokens, weight, preferred_element_type=jnp.float32).astype(jnp.bfloat16)
+    values, in_gate, out_gate = (
+        projected[:, j * own : (j + 1) * own].astype(jnp.float32) for j in range(3)
+    )
+    signal = in_gate * values
+    spec = dot32(table, signal)
+    resp = dot32(table, taps)
+    spec_re, spec_im, resp_re, resp_im = spec[:total], spec[total:], resp[:total], resp[total:]
+    prod = jnp.concatenate(
+        [spec_re * resp_re - spec_im * resp_im, -(spec_re * resp_im + spec_im * resp_re)]
+    )
+    conv = dot32(back, prod)
+    gated = (out_gate * (conv + gain[None, :] * signal)).astype(jnp.bfloat16)
+    mine = lax.all_to_all(gated.reshape(seq_size, row_count * own // 128, 128), "seq", split_axis=0, concat_axis=0, tiled=True)
+    whole = lax.all_gather(mine, "ch", axis=0, tiled=True)
+    whole = whole.reshape(-1, row_count, own).transpose(1, 0, 2).reshape(row_count, -1)
+    return jnp.dot(whole, out_weight, preferred_element_type=jnp.float32).astype(jnp.bfloat16)
+
+
 def solution(mesh):
     in_specs = (P("seq", None), P("seq", None, "ch"), P("seq", "ch"), P("ch"), P(None, "ch"))
     out_specs = P("seq", "ch")
-    return jax.shard_map(
-        per_device, mesh=mesh, in_specs=in_specs, out_specs=out_specs, check_vma=False
-    )
+
+    def whole(tokens, in_weight, filter_taps, skip_gain, out_weight):
+        dense = tokens.shape[0] <= DENSE_LIMIT
+        body = per_device if dense else per_device_long
+        return jax.shard_map(
+            body, mesh=mesh, in_specs=in_specs, out_specs=out_specs, check_vma=False
+        )(tokens, in_weight, filter_taps, skip_gain, out_weight)
+
+    return whole

time: 288 us -> 134 us (0.47)
  waiting for transfers between devices: 163 us -> 58.2 us
  matrix products: 35.7 us -> 12.9 us
  starting transfers between devices: 34.3 us -> 13.3 us
  local copies, waits for them, and re-layouts: 20.8 us -> 17.8 us
    all_gather x1, waiting for transfers between devices: 95.6 us -> 35.7 us  [per_device(): all_tokens = lax.all_gather(tokens, 'seq', axis=0, tiled=True)]
    all_to_all x8 -> x2, waiting for transfers between devices: 67 us -> 21.8 us  [the longest x1 21.8 us: per_device(): lax.all_to_all(in_weight.reshape(-1, 3, seq_size, own).transpose(2, 0, 1,...]
    dot_general x19 -> x5, matrix products: 34.5 us -> 10.7 us  [the longest x4 6.57 us: dot32(): jnp.dot(left.astype(jnp.bfloat16), right.astype(jnp.bfloat16), preferred_...]
    all_to_all x8 -> x2, starting transfers between devices: 34.3 us -> 13.3 us  [the longest x1 7.28 us: per_device(): lax.all_to_all(filter_taps.astype(jnp.bfloat16).reshape(row_count, seq_si...]
    all_to_all x10 -> x0, local copies, waits for them, and re-layouts: 6.62 us -> none  [the longest x1 1.89 us: per_device(): lax.all_to_all(sectioned[3], 'seq', split_axis=0, concat_axis=2, tiled=True)]
    transpose x0 -> x3, local copies, waits for them, and re-layouts: none -> 3.75 us  [the longest x1 2.44 us: per_device(): in_weight.reshape(-1, 3, seq_size, own).transpose(2, 0, 1, 3)]
  transfers between devices with their start and end apart: 9 -> 3, of which waited for: 8 -> 2; matrix products, arithmetic and copies ran while one was open for 11% -> 13% of each run, Pallas kernels for 0% -> 0%
where the time goes in v1:
time: 134 us; the launch traced here: 133 us
  waiting for transfers between devices  58.2 us (43%)
  local copies, waits for them, and re-layouts  17.8 us (13%)
  blocking collectives  17.6 us (13%)
  between operations  13.5 us (10%)
  starting transfers between devices  13.3 us (10%)
  matrix products  12.9 us (10%)
    all_gather x1, waiting for transfers between devices, per_device(): all_tokens = lax.all_gather(tokens, 'seq', axis=0, tiled=True)  35.7 us
    all_to_all x1, waiting for transfers between devices, per_device(): lax.all_to_all(in_weight.reshape(-1, 3, seq_size, own).transpose(2, 0, 1,...  21.8 us
    all_to_all x1, blocking collectives, per_device(): lax.all_to_all(gated.reshape(seq_size, row_count * own // 128, 128), 'seq...  10 us
    all_gather x1, blocking collectives, per_device(): whole = lax.all_gather(mine, 'ch', axis=0, tiled=True)  7.58 us
    all_to_all x1, starting transfers between devices, per_device(): lax.all_to_all(filter_taps.astype(jnp.bfloat16).reshape(row_count, seq_si...  7.28 us
    dot_general x4, matrix products, dot32(): jnp.dot(left.astype(jnp.bfloat16), right.astype(jnp.bfloat16), preferred_...  6.57 us
    all_to_all x1, starting transfers between devices, per_device(): lax.all_to_all(in_weight.reshape(-1, 3, seq_size, own).transpose(2, 0, 1,...  6.02 us
    reshape x1, local copies, waits for them, and re-layouts, per_device(): in_weight.reshape(-1, 3, seq_size, own).transpose(2, 0, 1, 3)  4.62 us
  transfers between devices with their start and end apart: 3, of which 2 were waited for; matrix products, arithmetic and copies ran while one was open for 13% of the time, Pallas kernels for 0%

profile of v1, /device:TPU:0, one launch (start us, length us, event | category | flops | bytes accessed | tf_op | source)
XLA Modules:
  0.0 133.3 jit_solution(4300170859172510660)
XLA Ops:
  6.5 0.0 copy-start
  6.5 0.7 all-gather.2.cloned.1.call-update
  7.3 1.1 copy.16
  8.3 0.2 copy.17
  8.5 0.8 reshape.32
  9.3 7.3 %all-to-all-start.1 = ((bf16[8,64,128]{2,1,0:T(8,128)(2,1)}), bf16[8,64,128]{2,1,0:T(8,128)(2,1)S(1)}, u32[]{:S(2)}, u32[]{:S(2)}) async-start(bf16[8,64,128]{2,1,0:T(8,128)(2,1)} %reshape.32), calls=%async_computation.1 | async-start | bytes 262144 | tf_op jit(solution)/shard_map/all_to_all | solution.py:159
  16.6 1.4 %copy.14 = bf16[256,3,512]{0,2,1:T(8,128)(2,1)S(1)} copy(bf16[256,3,512]{2,0,1:T(8,128)(2,1)} %param.8) | data formatting | bytes 1572864 | tf_op args[1]
  18.0 2.4 %copy.15 = bf16[8,256,3,64]{3,2,1,0:T(4,128)(2,1)} copy(bf16[8,256,3,64]{1,3,0,2:T(8,128)(2,1)S(1)} %bitcast.26) | data formatting | bytes 1572864 | tf_op jit(solution)/shard_map/transpose | solution.py:156
  20.5 4.6 %reshape.29 = bf16[8,384,128]{2,1,0:T(8,128)(2,1)} reshape(bf16[8,256,3,64]{3,2,1,0:T(4,128)(2,1)} %copy.15) | data formatting | bytes 1572864 | tf_op jit(solution)/shard_map/reshape | solution.py:156
  25.1 0.0 all-to-all-done.1
  25.1 6.0 %all-to-all-start = ((bf16[8,384,128]{2,1,0:T(8,128)(2,1)}), bf16[8,384,128]{2,1,0:T(8,128)(2,1)S(1)}, u32[]{:S(2)}, u32[]{:S(2)}) async-start(bf16[8,384,128]{2,1,0:T(8,128)(2,1)} %reshape.29), calls=%async_computation | async-start | bytes 1572864 | tf_op jit(solution)/shard_map/all_to_all | solution.py:155
  31.1 0.8 dynamic_slice.3
  31.9 0.8 reshape.33
  32.7 3.6 %fusion.10 = f32[2048,64]{0,1:T(8,128)S(1)} fusion(bf16[2048,1024]{1,0:T(8,128)(2,1)} %constant.16.clone, bf16[1024,64]{1,0:T(8,128)(2,1)} %reshape.33), kind=kOutput, calls=%fused_computation.15 | convolution fusion | flops 268435456 | bytes 4849664 | tf_op jit(solution)/shard_map/dot_general | solution.py:142
  36.3 21.8 %all-to-all-done = bf16[8,384,128]{2,1,0:T(8,128)(2,1)S(1)} async-done(((bf16[8,384,128]{2,1,0:T(8,128)(2,1)}), bf16[8,384,128]{2,1,0:T(8,128)(2,1)S(1)}, u32[]{:S(2)}, u32[]{:S(2)}) %all-to-all-start) | async-done | bytes 786464 | tf_op jit(solution)/shard_map/all_to_all | solution.py:155
  58.1 1.6 %reshape.30 = bf16[2048,192]{1,0:T(8,128)(2,1)} reshape(bf16[8,384,128]{2,1,0:T(8,128)(2,1)S(1)} %all-to-all-done) | data formatting | bytes 1572864 | tf_op jit(solution)/shard_map/reshape | solution.py:158
  59.7 35.7 %all-gather.2.cloned.1.call-done = bf16[1024,2048]{1,0:T(8,128)(2,1)} async-done(((bf16[128,2048]{1,0:T(8,128)(2,1)}), bf16[1024,2048]{1,0:T(8,128)(2,1)}) %all-gather.2.cloned.1.call-update) | async-done | bytes 4194320 | tf_op jit(solution)/shard_map/all_gather | solution.py:154
  95.4 4.2 %convolution_convert_fusion = bf16[1024,192]{0,1:T(8,128)(2,1)S(1)} fusion(bf16[1024,2048]{1,0:T(8,128)(2,1)} %all-gather.2.cloned.1.call-done, bf16[2048,192]{1,0:T(8,128)(2,1)} %reshape.30), kind=kOutput, calls=%fused_computation | convolution fusion | flops 805502976 | bytes 5373952 | tf_op jit(solution)/shard_map/dot_general | solution.py:164
  99.6 0.0 copy-done.1
  99.6 0.0 copy-start.3
  99.6 1.4 %fusion.6 = f32[2048,64]{0,1:T(8,128)S(1)} fusion(bf16[2048,1024]{1,0:T(8,128)(2,1)S(1)} %copy-done.1, bf16[1024,192]{0,1:T(8,128)(2,1)S(1)} %convolution_convert_fusion), kind=kOutput, calls=%fused_computation.12 | convolution fusion | flops 268697600 | bytes 4980736 | tf_op jit(solution)/shard_map/dot_general | solution.py:142
  101.0 0.2 copy-done.3
  101.2 0.8 fusion.5
  101.9 0.8 copy-done.2
  102.8 0.8 fusion.3
  103.6 0.2 copy.18
  103.7 0.1 reshape.34
  103.9 10.0 %all_to_all.15 = bf16[8,64,128]{2,1,0:T(8,128)(2,1)S(1)} all-to-all(bf16[8,64,128]{2,1,0:T(8,128)(2,1)S(1)} %reshape.34), channel_id=1, replica_groups=mesh['seq'=8,'ch'=4] {'seq'}, dimensions={0} | all-to-all | bytes 262144 | tf_op jit(solution)/shard_map/all_to_all | solution.py:177
  113.9 7.6 %all_gather.7 = bf16[32,64,128]{2,1,0:T(8,128)(2,1)} all-gather(bf16[8,64,128]{2,1,0:T(8,128)(2,1)S(1)} %all_to_all.15), channel_id=1, replica_groups=mesh['seq'=8,'ch'=4] {'ch'}, dimensions={0}, use_global_device_ids=true | all-gather | bytes 655360 | tf_op jit(solution)/shard_map/all_gather | solution.py:178
  121.5 1.6 %reshape.35 = bf16[32,128,64]{2,1,0:T(8,128)(2,1)S(1)} reshape(bf16[32,64,128]{2,1,0:T(8,128)(2,1)} %all_gather.7) | data formatting | bytes 1048576 | tf_op jit(solution)/shard_map/reshape | solution.py:179
  123.1 1.1 copy.19
  124.3 2.2 %convolution_convert_fusion.1 = bf16[128,512]{1,0:T(8,128)(2,1)} fusion(bf16[128,2048]{0,1:T(8,128)(2,1)} %bitcast.27, bf16[2048,512]{1,0:T(8,128)(2,1)S(1)} %copy-done), kind=kOutput, calls=%fused_computation.6 | convolution fusion | flops 268500992 | bytes 2752512 | tf_op jit(solution)/shard_map/dot_general | solution.py:180
  (4 shorter events, 0.0 us)
Async XLA Ops:
  6.5 117.7 %copy-start = (bf16[2048,512]{1,0:T(8,128)(2,1)S(1)}, bf16[2048,512]{1,0:T(8,128)(2,1)}, u32[]{:S(2)}) copy-start(bf16[2048,512]{1,0:T(8,128)(2,1)} %param.11) | copy-start | bytes 6291460
  6.5 88.9 %all-gather.2.cloned.1.call-start = ((), (), s32[]{:S(2)}) async-start(), calls=%async_computation.3 | async-start | bytes 4718592 | tf_op jit(solution)/shard_map/all_gather | solution.py:154
  9.3 15.8 %all-to-all-start.1 = ((bf16[8,64,128]{2,1,0:T(8,128)(2,1)}), bf16[8,64,128]{2,1,0:T(8,128)(2,1)S(1)}, u32[]{:S(2)}, u32[]{:S(2)}) async-start(bf16[8,64,128]{2,1,0:T(8,128)(2,1)} %reshape.32), calls=%async_computation.1 | async-start | bytes 262144 | tf_op jit(solution)/shard_map/all_to_all | solution.py:159
  25.1 33.0 %all-to-all-start = ((bf16[8,384,128]{2,1,0:T(8,128)(2,1)}), bf16[8,384,128]{2,1,0:T(8,128)(2,1)S(1)}, u32[]{:S(2)}, u32[]{:S(2)}) async-start(bf16[8,384,128]{2,1,0:T(8,128)(2,1)} %reshape.29), calls=%async_computation | async-start | bytes 1572864 | tf_op jit(solution)/shard_map/all_to_all | solution.py:155
  95.4 4.2 %copy-start.1 = (bf16[2048,1024]{1,0:T(8,128)(2,1)S(1)}, bf16[2048,1024]{1,0:T(8,128)(2,1)}, u32[]{:S(2)}) copy-start(bf16[2048,1024]{1,0:T(8,128)(2,1)} %constant.16.clone) | copy-start | bytes 12582916
  99.6 1.6 %copy-start.3 = (bf16[1024,1024]{1,0:T(8,128)(2,1)S(1)}, bf16[1024,1024]{1,0:T(8,128)(2,1)}, u32[]{:S(2)}) copy-start(bf16[1024,1024]{1,0:T(8,128)(2,1)} %constant.18) | copy-start | bytes 6291460
  101.2 1.6 %copy-start.2 = (bf16[1024,1024]{1,0:T(8,128)(2,1)S(1)}, bf16[1024,1024]{1,0:T(8,128)(2,1)}, u32[]{:S(2)}) copy-start(bf16[1024,1024]{1,0:T(8,128)(2,1)} %constant.19) | copy-start | bytes 6291460
Sparse Core Ops, SparseCore 0:
  9.5 85.8 all-gather.1

commit v2 on v1

--- a/solution.py
+++ b/solution.py
@@ -4,6 +4,8 @@
 import jax.numpy as jnp
 import numpy as np
 from jax import lax
+from jax.experimental import pallas as pl
+from jax.experimental.pallas import tpu as pltpu
 from jax.sharding import PartitionSpec as P
 
 HIGHEST_PREC = lax.Precision.HIGHEST
@@ -180,13 +182,318 @@
     return jnp.dot(whole, out_weight, preferred_element_type=jnp.float32).astype(jnp.bfloat16)
 
 
+def fused_kernel(
+    tokens, weight, taps, gain, out_weight, table_hbm, back_hbm, out,
+    all_tokens, pack_w, recv_w, full_w, pack_f, recv_f, all_taps, table, back, mix_w,
+    resp, signal, split, out_gate, prod, pack_g, recv_g, wide,
+    local_sem, w_send, w_recv, f_send, f_recv, up_send, down_send, z_recv, y_send, y_recv,
+    c_send, c_recv, x_send, x_recv, k_send, k_recv, g_send, g_recv, h_send, h_recv,
+):
+    f32, bf16 = jnp.float32, jnp.bfloat16
+    me, ch = lax.axis_index("seq"), lax.axis_index("ch")
+    z, y = me // 2, me % 2
+    rows, depth = tokens.shape[0], tokens.shape[1]
+    part = rows // 4
+    total = rows * 8
+    half = rows // 2
+    w_rows = weight.shape[0]
+    chans = weight.shape[1] // 3
+    own = chans // 8
+
+    def flip(value, bit):
+        return value + bit - 2 * bit * (value // bit % 2)
+
+    x_ch, c_ch, d_ch = flip(ch, 2), flip(ch, 1), flip(flip(ch, 2), 1)
+    mates = (c_ch, x_ch, d_ch)
+
+    barrier = pltpu.get_barrier_semaphore()
+    for k in range(1, 8):
+        pl.semaphore_signal(
+            barrier, inc=1, device_id={"seq": (me + k) % 8, "ch": ch},
+            device_id_type=pl.DeviceIdType.MESH,
+        )
+    for mate in mates:
+        pl.semaphore_signal(
+            barrier, inc=1, device_id={"seq": me, "ch": mate}, device_id_type=pl.DeviceIdType.MESH
+        )
+
+    own_rows = pl.ds(pl.multiple_of(me * rows, rows), rows)
+    loads = [
+        pltpu.make_async_copy(tokens, all_tokens.at[own_rows, :], local_sem.at[0]),
+        pltpu.make_async_copy(table_hbm, table, local_sem.at[1]),
+        pltpu.make_async_copy(back_hbm, back, local_sem.at[2]),
+        pltpu.make_async_copy(out_weight, mix_w, local_sem.at[3]),
+    ]
+
+    for p in range(8):
+        lanes = slice(p * own, (p + 1) * own)
+        pack_f[p] = jnp.concatenate([taps[:half, lanes], taps[half:, lanes]], axis=1).astype(bf16)
+        pack_w[p, :w_rows] = jnp.concatenate(
+            [weight[:, lanes], weight[:, chans + p * own : chans + (p + 1) * own]], axis=1
+        )
+        last = slice(2 * chans + p * own, 2 * chans + (p + 1) * own)
+        pack_w[p, w_rows:] = jnp.concatenate(
+            [weight[: w_rows // 2, last], weight[w_rows // 2 :, last]], axis=1
+        )
+
+    pl.semaphore_wait(barrier, 10)
+
+    def remote(source, target, send, recv, seq_id, ch_id):
+        return pltpu.make_async_remote_copy(
+            src_ref=source, dst_ref=target, send_sem=send, recv_sem=recv,
+            device_id={"seq": seq_id, "ch": ch_id}, device_id_type=pl.DeviceIdType.MESH,
+        )
+
+    def piece(seq_id, quarter):
+        start = pl.multiple_of(seq_id * rows + quarter * part, part)
+        return all_tokens.at[pl.ds(start, part), :]
+
+    mine = tokens.at[pl.ds(pl.multiple_of(ch * part, part), part), :]
+
+    def guarded(condition, action):
+        if condition is None:
+            action()
+        else:
+            pl.when(condition)(action)
+
+    sent = []
+
+    def send(condition, copy):
+        guarded(condition, lambda: copy().start())
+        sent.append((condition, copy))
+
+    def z_copy(source, zs, step):
+        sems = up_send if step > 0 else down_send
+        return lambda: remote(source(), piece(2 * zs + y, ch), sems.at[zs], z_recv.at[zs], me + 2 * step, ch)
+
+    def y_copy(source, zs):
+        return lambda: remote(source(), piece(2 * zs + y, ch), y_send.at[zs], y_recv.at[zs], flip(me, 1), ch)
+
+    send(z < 3, z_copy(lambda: mine, z, 1))
+    send(z > 0, z_copy(lambda: mine, z, -1))
+    send(None, y_copy(lambda: mine, z))
+
+    def w_copy(k):
+        p = (me + k) % 8
+        return lambda: remote(pack_w.at[p], recv_w.at[me], w_send.at[k], w_recv.at[me], p, ch)
+
+    def f_copy(k):
+        p = (me + k) % 8
+        return lambda: remote(pack_f.at[p], recv_f.at[me], f_send.at[k], f_recv.at[me], p, ch)
+
+    order = (4, 3, 5, 2, 6, 1, 7)
+    for k in order:
+        send(None, f_copy(k))
+    for k in order:
+        send(None, w_copy(k))
+    for load in loads:
+        load.start()
+    recv_w[me] = pack_w[me]
+    recv_f[me] = pack_f[me]
+
+    def spread(condition, s):
+        send(condition, lambda: remote(piece(s, ch), piece(s, ch), c_send.at[s], c_recv.at[s], me, c_ch))
+        send(condition, lambda: remote(piece(s, ch), piece(s, ch), x_send.at[s], x_recv.at[s], me, x_ch))
+
+    def from_z(condition, zs, step):
+        s = 2 * zs + y
+        guarded(condition, lambda: z_copy(lambda: piece(s, ch), zs, step)().wait_recv())
+        onward = (z < 3) if step > 0 else (z > 0)
+        send(jnp.logical_and(condition, onward), z_copy(lambda: piece(s, ch), zs, step))
+        send(condition, y_copy(lambda: piece(s, ch), zs))
+        spread(condition, s)
+
+    def from_y(condition, zs):
+        s = 2 * zs + 1 - y
+        guarded(condition, lambda: remote(
+            piece(s, ch), piece(s, ch), y_send.at[zs], y_recv.at[zs], flip(me, 1), ch).wait_recv())
+        spread(condition, s)
+
+    def from_x(condition, s):
+        guarded(condition, lambda: remote(
+            piece(s, x_ch), piece(s, x_ch), x_send.at[s], x_recv.at[s], me, x_ch).wait_recv())
+        send(condition, lambda: remote(
+            piece(s, x_ch), piece(s, x_ch), k_send.at[s], k_recv.at[s], me, c_ch))
+
+    from_y(None, z)
+    arrived = [(None, 2 * z + 1 - y)]
+    for d in range(1, 4):
+        below, above = z >= d, z + d <= 3
+        from_z(below, z - d, 1)
+        from_z(above, z + d, -1)
+        while arrived:
+            from_x(*arrived.pop(0))
+        from_y(below, z - d)
+        from_y(above, z + d)
+        for condition, zs in ((below, z - d), (above, z + d)):
+            arrived += [(condition, 2 * zs + y), (condition, 2 * zs + 1 - y)]
+        if d == 1:
+            taps_phase(me, ch, remote, recv_f, f_send, f_recv, all_taps, half, own, loads, table, resp)
+    while arrived:
+        from_x(*arrived.pop(0))
+
+    for k in range(1, 8):
+        s = (me + k) % 8
+        remote(recv_w.at[s], recv_w.at[s], w_send.at[k], w_recv.at[s], s, ch).wait_recv()
+    for s in range(8):
+        base = s * w_rows
+        full_w[base : base + w_rows, : 2 * own] = recv_w[s, :w_rows]
+        full_w[base : base + w_rows // 2, 2 * own :] = recv_w[s, w_rows:][:, :own]
+        full_w[base + w_rows // 2 : base + w_rows, 2 * own :] = recv_w[s, w_rows:][:, own:]
+
+    for k in range(1, 8):
+        s = (me + k) % 8
+        remote(piece(s, c_ch), piece(s, c_ch), c_send.at[s], c_recv.at[s], me, c_ch).wait_recv()
+        remote(piece(s, d_ch), piece(s, d_ch), k_send.at[s], k_recv.at[s], me, c_ch).wait_recv()
+    loads[0].wait()
+
+    @pl.loop(0, total // 256)
+    def _(i):
+        at = pl.ds(pl.multiple_of(i * 256, 256), 256)
+        proj = jnp.dot(all_tokens[at, :], full_w[...], preferred_element_type=f32)
+        proj = proj.astype(bf16).astype(f32)
+        sig = proj[:, own : 2 * own] * proj[:, :own]
+        signal[at, :] = sig
+        out_gate[at, :] = proj[:, 2 * own :]
+        high = sig.astype(bf16)
+        split[at, :] = jnp.concatenate([high, (sig - high.astype(f32)).astype(bf16)], axis=1)
+
+    @pl.loop(0, total // 256)
+    def _(i):
+        at = pl.ds(pl.multiple_of(i * 256, 256), 256)
+        under = pl.ds(pl.multiple_of(total + i * 256, 256), 256)
+        re = jnp.dot(table[at, :], split[...], preferred_element_type=f32)
+        im = jnp.dot(table[under, :], split[...], preferred_element_type=f32)
+        re, im = re[:, :own] + re[:, own:], im[:, :own] + im[:, own:]
+        filt_re, filt_im = resp[at, :], resp[under, :]
+        prod[at, :] = (re * filt_re - im * filt_im).astype(bf16)
+        prod[under, :] = (re * filt_im + im * filt_re).astype(bf16)
+
+    skip = jnp.zeros((1, own), f32)
+    for p in range(8):
+        skip = skip + jnp.where(me == p, gain[:, p * own : (p + 1) * own], 0.0)
+
+    loads[2].wait()
+
+    def g_copy(k):
+        p = (me + k) % 8
+        return lambda: remote(pack_g.at[p], recv_g.at[ch, me], g_send.at[k], g_recv.at[me], p, ch)
+
+    for k in (4, 3, 5, 2, 6, 1, 7, 0):
+        p = (me + k) % 8
+        at = pl.ds(pl.multiple_of(p * rows, rows), rows)
+        conv = jnp.dot(back[at, :], prod[...], preferred_element_type=f32)
+        gated = (out_gate[at, :] * (conv + skip * signal[at, :])).astype(bf16)
+        packed = jnp.concatenate([gated[:half], gated[half:]], axis=1)
+        if k:
+            pack_g[p] = packed
+            send(None, g_copy(k))
+        else:
+            recv_g[ch, me] = packed
+
+    def h_copy(j, s):
+        return lambda: remote(recv_g.at[ch, s], recv_g.at[ch, s], h_send.at[j, s], h_recv.at[j, s], me, mates[j])
+
+    for k in (0, 1, 7, 2, 6, 3, 5, 4):
+        s = (me + k) % 8
+        if k:
+            remote(recv_g.at[ch, s], recv_g.at[ch, s], g_send.at[k], g_recv.at[s], s, ch).wait_recv()
+        for j in (2, 1, 0):
+            send(None, h_copy(j, s))
+    loads[3].wait()
+    for j in range(3):
+        for s in range(8):
+            remote(
+                recv_g.at[mates[j], s], recv_g.at[mates[j], s], h_send.at[j, s], h_recv.at[j, s], me, mates[j]
+            ).wait_recv()
+    for c in range(4):
+        for s in range(0, 8, 2):
+            base = (c * 8 + s) * own
+            a, b = recv_g[c, s], recv_g[c, s + 1]
+            wide[:half, base : base + 2 * own] = jnp.concatenate([a[:, :own], b[:, :own]], axis=1)
+            wide[half:, base : base + 2 * own] = jnp.concatenate([a[:, own:], b[:, own:]], axis=1)
+    out[...] = jnp.dot(wide[...], mix_w[...], preferred_element_type=f32).astype(bf16)
+    for condition, copy in sent:
+        guarded(condition, lambda copy=copy: copy().wait_send())
+
+
+def taps_phase(me, ch, remote, recv_f, f_send, f_recv, all_taps, half, own, loads, table, resp):
+    for k in range(1, 8):
+        s = (me + k) % 8
+        remote(recv_f.at[s], recv_f.at[s], f_send.at[k], f_recv.at[s], s, ch).wait_recv()
+    for s in range(8):
+        base = 2 * s * half
+        all_taps[base : base + half, :] = recv_f[s][:, :own]
+        all_taps[base + half : base + 2 * half, :] = recv_f[s][:, own:]
+    loads[1].wait()
+
+    @pl.loop(0, table.shape[0] // 256)
+    def _(i):
+        at = pl.ds(pl.multiple_of(i * 256, 256), 256)
+        resp[at, :] = jnp.dot(table[at, :], all_taps[...], preferred_element_type=jnp.float32)
+
+
+def per_device_fused(tokens, in_weight, filter_taps, skip_gain, out_weight):
+    rows, depth = tokens.shape
+    w_rows, _, chans = in_weight.shape
+    own = chans // 8
+    total = 8 * rows
+    width = out_weight.shape[1]
+    cos_table, sin_table = half_step_tables(total)
+    table = jnp.asarray(np.concatenate([cos_table, sin_table]), jnp.bfloat16)
+    back = jnp.asarray(np.concatenate([cos_table.T, sin_table.T], axis=1) / total, jnp.bfloat16)
+    f32, bf16 = jnp.float32, jnp.bfloat16
+    vmem, anywhere = pl.BlockSpec(memory_space=pltpu.VMEM), pl.BlockSpec(memory_space=pl.ANY)
+    dma = pltpu.SemaphoreType.DMA
+    return pl.pallas_call(
+        fused_kernel,
+        out_shape=jax.ShapeDtypeStruct((rows, width), bf16),
+        in_specs=[anywhere, vmem, vmem, vmem, anywhere, anywhere, anywhere],
+        out_specs=vmem,
+        scratch_shapes=[
+            pltpu.VMEM((total, depth), bf16),
+            pltpu.VMEM((8, w_rows * 3 // 2, 2 * own), bf16),
+            pltpu.VMEM((8, w_rows * 3 // 2, 2 * own), bf16),
+            pltpu.VMEM((8 * w_rows, 3 * own), bf16),
+            pltpu.VMEM((8, rows // 2, 2 * own), bf16),
+            pltpu.VMEM((8, rows // 2, 2 * own), bf16),
+            pltpu.VMEM((total, own), bf16),
+            pltpu.VMEM((2 * total, total), bf16),
+            pltpu.VMEM((total, 2 * total), bf16),
+            pltpu.VMEM(out_weight.shape, bf16),
+            pltpu.VMEM((2 * total, own), f32),
+            pltpu.VMEM((total, own), f32),
+            pltpu.VMEM((total, 2 * own), bf16),
+            pltpu.VMEM((total, own), f32),
+            pltpu.VMEM((2 * total, own), bf16),
+            pltpu.VMEM((8, rows // 2, 2 * own), bf16),
+            pltpu.VMEM((4, 8, rows // 2, 2 * own), bf16),
+            pltpu.VMEM((rows, out_weight.shape[0]), bf16),
+            dma((4,)), dma((8,)), dma((8,)), dma((8,)), dma((8,)),
+            dma((4,)), dma((4,)), dma((4,)), dma((4,)), dma((4,)),
+            dma((8,)), dma((8,)), dma((8,)), dma((8,)), dma((8,)), dma((8,)),
+            dma((8,)), dma((8,)), dma((3, 8)), dma((3, 8)),
+        ],
+        compiler_params=pltpu.CompilerParams(
+            collective_id=0, has_side_effects=True, vmem_limit_bytes=50 * 2**20
+        ),
+    )(
+        tokens, in_weight.reshape(w_rows, 3 * chans), filter_taps, skip_gain[None, :],
+        out_weight, table, back,
+    )
+
+
 def solution(mesh):
     in_specs = (P("seq", None), P("seq", None, "ch"), P("seq", "ch"), P("ch"), P(None, "ch"))
     out_specs = P("seq", "ch")
 
     def whole(tokens, in_weight, filter_taps, skip_gain, out_weight):
-        dense = tokens.shape[0] <= DENSE_LIMIT
-        body = per_device if dense else per_device_long
+        fits = mesh.shape["seq"] == 8 and mesh.shape["ch"] == 4
+        fits = fits and tokens.shape[0] == 1024 and filter_taps.shape[1] == 2048
+        if fits:
+            body = per_device_fused
+        else:
+            body = per_device if tokens.shape[0] <= DENSE_LIMIT else per_device_long
         return jax.shard_map(
             body, mesh=mesh, in_specs=in_specs, out_specs=out_specs, check_vma=False
         )(tokens, in_weight, filter_taps, skip_gain, out_weight)

time: 134 us -> 71.1 us (0.53)
  Pallas kernels: 0 us -> 63.6 us
  waiting for transfers between devices: 58.2 us -> 0 us
  blocking collectives: 17.6 us -> 0 us
  between operations: 13.5 us -> 0.03 us
  starting transfers between devices: 13.3 us -> 0 us
  matrix products: 12.9 us -> 0 us
  local copies, waits for them, and re-layouts: 17.8 us -> 7.18 us
    pallas_call x0 -> x1, Pallas kernels: none -> 63.6 us  [per_device_fused(): pl.pallas_call(fused_kernel, out_shape=jax.ShapeDtypeStruct((rows, width)...]
    all_gather x1 -> x0, waiting for transfers between devices: 35.7 us -> none  [per_device(): all_tokens = lax.all_gather(tokens, 'seq', axis=0, tiled=True)]
    all_to_all x2 -> x0, waiting for transfers between devices: 21.8 us -> none  [the longest x1 21.8 us: per_device(): lax.all_to_all(in_weight.reshape(-1, 3, seq_size, own).transpose(2, 0, 1,...]
    all_to_all x2 -> x0, starting transfers between devices: 13.3 us -> none  [the longest x1 7.28 us: per_device(): lax.all_to_all(filter_taps.astype(jnp.bfloat16).reshape(row_count, seq_si...]
    dot_general x6 -> x0, matrix products: 12.9 us -> none  [the longest x4 6.57 us: dot32(): jnp.dot(left.astype(jnp.bfloat16), right.astype(jnp.bfloat16), preferred_...]
    all_to_all x1 -> x0, blocking collectives: 10 us -> none  [per_device(): lax.all_to_all(gated.reshape(seq_size, row_count * own // 128, 128), 'seq...]
    reshape x6 -> x1, local copies, waits for them, and re-layouts: 9.63 us -> 1.41 us  [per_device_fused(): in_weight.reshape(w_rows, 3 * chans)]
    all_gather x1 -> x0, blocking collectives: 7.58 us -> none  [per_device(): whole = lax.all_gather(mine, 'ch', axis=0, tiled=True)]
  transfers between devices with their start and end apart: 3 -> 0, of which waited for: 2 -> 0; matrix products, arithmetic and copies ran while one was open for 13% -> 0% of each run, Pallas kernels for 0% -> 0%
where the time goes in v2:
time: 71.1 us; the launch traced here: 70.8 us
  Pallas kernels  63.6 us (89%)
  local copies, waits for them, and re-layouts  7.18 us (10%)
    pallas_call x1, Pallas kernels, per_device_fused(): pl.pallas_call(fused_kernel, out_shape=jax.ShapeDtypeStruct((rows, width)...  63.6 us
    unnamed x10, local copies, waits for them, and re-layouts  5.77 us

profile of v2, /device:TPU:0, one launch (start us, length us, event | category | flops | bytes accessed | tf_op | source)
XLA Modules:
  0.0 70.8 jit_solution(6869415182403485778)
XLA Ops:
  0.0 0.0 copy-start
  0.0 2.4 %copy.9 = bf16[256,3,512]{0,2,1:T(8,128)(2,1)} copy(bf16[256,3,512]{2,0,1:T(8,128)(2,1)} %param.8) | data formatting | bytes 1572864 | tf_op args[1]
  2.4 1.4 %copy.10.weight = bf16[256,1536]{1,0:T(8,128)(2,1)S(1)} copy(bf16[256,1536]{0,1:T(8,128)(2,1)} %bitcast.3) | data formatting | bytes 1572864 | tf_op jit(solution)/shard_map/reshape | solution.py:481
  3.9 0.0 copy-done
  3.9 0.0 copy-start.1
  3.9 1.0 %copy-done.1 = bf16[128,2048]{1,0:T(8,128)(2,1)S(1)} copy-done((bf16[128,2048]{1,0:T(8,128)(2,1)S(1)}, bf16[128,2048]{1,0:T(8,128)(2,1)}, u32[]{:S(2)}) %copy-start.1) | copy-done | bytes 524312
  4.9 0.0 copy-start.2
  4.9 0.9 %copy-done.2 = f32[128,512]{1,0:T(8,128)S(1)} copy-done((f32[128,512]{1,0:T(8,128)S(1)}, f32[128,512]{1,0:T(8,128)}, u32[]{:S(2)}) %copy-start.2) | copy-done | bytes 262168
  5.9 0.0 copy-start.3
  5.9 0.7 copy-done.3
  6.5 63.6 %shard_map.73 = bf16[128,512]{1,0:T(8,128)(2,1)S(1)} custom-call(bf16[128,2048]{1,0:T(8,128)(2,1)S(1)} %copy-done.1, bf16[256,1536]{1,0:T(8,128)(2,1)S(1)} %copy.10.weight, f32[128,512]{1,0:T(8,128)S(1)} %copy-done.2, f32[1,512]{1,0:T(1,128)S(1)} %bitcast.2, bf16[2048,512]{1,0:T(8,128)(2,1)S(1)} %copy-done, bf16[2048,1024]{1,0:T(8,128)(2,1)} %constant.4.clone.table_hbm, ...), custom_call_target="tpu_custom_call" | custom-call | tf_op jit(solution)/shard_map/pallas_call | solution.py:448
  70.2 0.7 copy.12
Async XLA Ops:
  0.0 3.9 %copy-start = (bf16[2048,512]{1,0:T(8,128)(2,1)S(1)}, bf16[2048,512]{1,0:T(8,128)(2,1)}, u32[]{:S(2)}) copy-start(bf16[2048,512]{1,0:T(8,128)(2,1)} %out_weight.1) | copy-start | bytes 6291460
  3.9 1.0 %copy-start.1 = (bf16[128,2048]{1,0:T(8,128)(2,1)S(1)}, bf16[128,2048]{1,0:T(8,128)(2,1)}, u32[]{:S(2)}) copy-start(bf16[128,2048]{1,0:T(8,128)(2,1)} %tokens.1) | copy-start | bytes 1572868
  4.9 0.9 %copy-start.2 = (f32[128,512]{1,0:T(8,128)S(1)}, f32[128,512]{1,0:T(8,128)}, u32[]{:S(2)}) copy-start(f32[128,512]{1,0:T(8,128)} %taps.1) | copy-start | bytes 786436
  5.9 0.7 copy-start.3

commit v3 on v2

--- a/solution.py
+++ b/solution.py
@@ -1,3 +1,4 @@
+import functools
 import math
 
 import jax
@@ -183,7 +184,8 @@
 
 
 def fused_kernel(
-    tokens, weight, taps, gain, out_weight, table_hbm, back_hbm, out,
+    tokens, weight_hbm, taps_hbm, gain_hbm, out_weight, table_hbm, back_hbm, out,
+    weight, taps, gain,
     all_tokens, pack_w, recv_w, full_w, pack_f, recv_f, all_taps, table, back, mix_w,
     resp, signal, split, out_gate, prod, pack_g, recv_g, wide,
     local_sem, w_send, w_recv, f_send, f_recv, up_send, down_send, z_recv, y_send, y_recv,
@@ -196,8 +198,7 @@
     part = rows // 4
     total = rows * 8
     half = rows // 2
-    w_rows = weight.shape[0]
-    chans = weight.shape[1] // 3
+    w_rows, chans = weight.shape[1:]
     own = chans // 8
 
     def flip(value, bit):
@@ -206,6 +207,13 @@
     x_ch, c_ch, d_ch = flip(ch, 2), flip(ch, 1), flip(flip(ch, 2), 1)
     mates = (c_ch, x_ch, d_ch)
 
+    first_loads = [
+        pltpu.make_async_copy(weight_hbm, weight, local_sem.at[4]),
+        pltpu.make_async_copy(taps_hbm, taps, local_sem.at[5]),
+        pltpu.make_async_copy(gain_hbm, gain, local_sem.at[6]),
+    ]
+    for load in first_loads:
+        load.start()
     barrier = pltpu.get_barrier_semaphore()
     for k in range(1, 8):
         pl.semaphore_signal(
@@ -225,15 +233,14 @@
         pltpu.make_async_copy(out_weight, mix_w, local_sem.at[3]),
     ]
 
+    for load in first_loads:
+        load.wait()
     for p in range(8):
         lanes = slice(p * own, (p + 1) * own)
         pack_f[p] = jnp.concatenate([taps[:half, lanes], taps[half:, lanes]], axis=1).astype(bf16)
-        pack_w[p, :w_rows] = jnp.concatenate(
-            [weight[:, lanes], weight[:, chans + p * own : chans + (p + 1) * own]], axis=1
-        )
-        last = slice(2 * chans + p * own, 2 * chans + (p + 1) * own)
+        pack_w[p, :w_rows] = jnp.concatenate([weight[0, :, lanes], weight[1, :, lanes]], axis=1)
         pack_w[p, w_rows:] = jnp.concatenate(
-            [weight[: w_rows // 2, last], weight[w_rows // 2 :, last]], axis=1
+            [weight[2, : w_rows // 2, lanes], weight[2, w_rows // 2 :, lanes]], axis=1
         )
 
     pl.semaphore_wait(barrier, 10)
@@ -284,8 +291,14 @@
     order = (4, 3, 5, 2, 6, 1, 7)
     for k in order:
         send(None, f_copy(k))
-    for k in order:
-        send(None, w_copy(k))
+    pending = list(order)
+
+    def more(count):
+        for k in pending[:count]:
+            send(None, w_copy(k))
+        del pending[:count]
+
+    more(1)
     for load in loads:
         load.start()
     recv_w[me] = pack_w[me]
@@ -315,22 +328,31 @@
         send(condition, lambda: remote(
             piece(s, x_ch), piece(s, x_ch), k_send.at[s], k_recv.at[s], me, c_ch))
 
+    tiles = [functools.partial(taps_tile, i, table, all_taps, resp) for i in range(8)]
     from_y(None, z)
+    more(1)
     arrived = [(None, 2 * z + 1 - y)]
     for d in range(1, 4):
         below, above = z >= d, z + d <= 3
         from_z(below, z - d, 1)
         from_z(above, z + d, -1)
-        while arrived:
-            from_x(*arrived.pop(0))
+        more(1)
+        if d == 1:
+            taps_arrive(me, ch, remote, recv_f, f_send, f_recv, all_taps, half, own)
+            loads[1].wait()
+        else:
+            tiles.pop(0)()
         from_y(below, z - d)
+        tiles.pop(0)()
         from_y(above, z + d)
+        more(1)
+        tiles.pop(0)()
         for condition, zs in ((below, z - d), (above, z + d)):
             arrived += [(condition, 2 * zs + y), (condition, 2 * zs + 1 - y)]
-        if d == 1:
-            taps_phase(me, ch, remote, recv_f, f_send, f_recv, all_taps, half, own, loads, table, resp)
     while arrived:
         from_x(*arrived.pop(0))
+    while tiles:
+        tiles.pop(0)()
 
     for k in range(1, 8):
         s = (me + k) % 8
@@ -417,7 +439,7 @@
         guarded(condition, lambda copy=copy: copy().wait_send())
 
 
-def taps_phase(me, ch, remote, recv_f, f_send, f_recv, all_taps, half, own, loads, table, resp):
+def taps_arrive(me, ch, remote, recv_f, f_send, f_recv, all_taps, half, own):
     for k in range(1, 8):
         s = (me + k) % 8
         remote(recv_f.at[s], recv_f.at[s], f_send.at[k], f_recv.at[s], s, ch).wait_recv()
@@ -425,12 +447,11 @@
         base = 2 * s * half
         all_taps[base : base + half, :] = recv_f[s][:, :own]
         all_taps[base + half : base + 2 * half, :] = recv_f[s][:, own:]
-    loads[1].wait()
-
-    @pl.loop(0, table.shape[0] // 256)
-    def _(i):
-        at = pl.ds(pl.multiple_of(i * 256, 256), 256)
-        resp[at, :] = jnp.dot(table[at, :], all_taps[...], preferred_element_type=jnp.float32)
+
+
+def taps_tile(i, table, all_taps, resp):
+    at = slice(i * 256, i * 256 + 256)
+    resp[at, :] = jnp.dot(table[at, :], all_taps[...], preferred_element_type=jnp.float32)
 
 
 def per_device_fused(tokens, in_weight, filter_taps, skip_gain, out_weight):
@@ -448,9 +469,12 @@
     return pl.pallas_call(
         fused_kernel,
         out_shape=jax.ShapeDtypeStruct((rows, width), bf16),
-        in_specs=[anywhere, vmem, vmem, vmem, anywhere, anywhere, anywhere],
+        in_specs=[anywhere] * 7,
         out_specs=vmem,
         scratch_shapes=[
+            pltpu.VMEM((3, w_rows, chans), bf16),
+            pltpu.VMEM((rows, chans), f32),
+            pltpu.VMEM((1, chans), f32),
             pltpu.VMEM((total, depth), bf16),
             pltpu.VMEM((8, w_rows * 3 // 2, 2 * own), bf16),
             pltpu.VMEM((8, w_rows * 3 // 2, 2 * own), bf16),
@@ -469,16 +493,16 @@
             pltpu.VMEM((8, rows // 2, 2 * own), bf16),
             pltpu.VMEM((4, 8, rows // 2, 2 * own), bf16),
             pltpu.VMEM((rows, out_weight.shape[0]), bf16),
-            dma((4,)), dma((8,)), dma((8,)), dma((8,)), dma((8,)),
+            dma((7,)), dma((8,)), dma((8,)), dma((8,)), dma((8,)),
             dma((4,)), dma((4,)), dma((4,)), dma((4,)), dma((4,)),
             dma((8,)), dma((8,)), dma((8,)), dma((8,)), dma((8,)), dma((8,)),
             dma((8,)), dma((8,)), dma((3, 8)), dma((3, 8)),
         ],
         compiler_params=pltpu.CompilerParams(
-            collective_id=0, has_side_effects=True, vmem_limit_bytes=50 * 2**20
+            collective_id=0, has_side_effects=True, vmem_limit_bytes=60 * 2**20
         ),
     )(
-        tokens, in_weight.reshape(w_rows, 3 * chans), filter_taps, skip_gain[None, :],
+        tokens, in_weight.transpose(1, 0, 2), filter_taps, skip_gain[None, :],
         out_weight, table, back,
     )
 

time: 71.1 us -> 61.5 us (0.86)
  local copies, waits for them, and re-layouts: 7.18 us -> 1.57 us
  Pallas kernels: 63.6 us -> 59.8 us
    unnamed x10 -> x1, local copies, waits for them, and re-layouts: 5.77 us -> 1.57 us
    pallas_call x1, Pallas kernels: 63.6 us -> 59.8 us  [per_device_fused(): pl.pallas_call(fused_kernel, out_shape=jax.ShapeDtypeStruct((rows, width)...]
    reshape x1 -> x0, local copies, waits for them, and re-layouts: 1.41 us -> none  [per_device_fused(): in_weight.reshape(w_rows, 3 * chans)]
where the time goes in v3:
time: 61.5 us; the launch traced here: 61.4 us
  Pallas kernels  59.8 us (97%)
  local copies, waits for them, and re-layouts  1.57 us (3%)
    pallas_call x1, Pallas kernels, per_device_fused(): pl.pallas_call(fused_kernel, out_shape=jax.ShapeDtypeStruct((rows, width)...  59.8 us
    unnamed x1, local copies, waits for them, and re-layouts  1.57 us

profile of v3, /device:TPU:0, one launch (start us, length us, event | category | flops | bytes accessed | tf_op | source)
XLA Modules:
  0.0 61.4 jit_solution(6731018930468133974)
XLA Ops:
  0.0 59.8 %shard_map.73 = bf16[128,512]{1,0:T(8,128)(2,1)} custom-call(bf16[128,2048]{1,0:T(8,128)(2,1)} %tokens.1, bf16[3,256,512]{2,1,0:T(8,128)(2,1)} %bitcast.2, f32[128,512]{1,0:T(8,128)} %taps_hbm.1, f32[1,512]{1,0:T(1,128)} %bitcast.3, bf16[2048,512]{1,0:T(8,128)(2,1)} %out_weight.1, bf16[2048,1024]{1,0:T(8,128)(2,1)} %constant.4.clone.table_hbm, ...), custom_call_target="tpu_custom_call" | custom-call | tf_op jit(solution)/shard_map/pallas_call | solution.py:469
  59.8 1.6 %copy.9 = bf16[128,512]{1,0:T(8,128)(2,1)} copy(bf16[128,512]{1,0:T(8,128)(2,1)} %shard_map.73) | data formatting | bytes 262144

commit v4 on v3

--- a/solution.py
+++ b/solution.py
@@ -288,7 +288,7 @@
         p = (me + k) % 8
         return lambda: remote(pack_f.at[p], recv_f.at[me], f_send.at[k], f_recv.at[me], p, ch)
 
-    order = (4, 3, 5, 2, 6, 1, 7)
+    order = (1, 7, 2, 6, 3, 5, 4)
     for k in order:
         send(None, f_copy(k))
     pending = list(order)
@@ -420,10 +420,17 @@
         s = (me + k) % 8
         if k:
             remote(recv_g.at[ch, s], recv_g.at[ch, s], g_send.at[k], g_recv.at[s], s, ch).wait_recv()
-        for j in (2, 1, 0):
+        for j in (1, 0):
             send(None, h_copy(j, s))
+    for k in (0, 1, 7, 2, 6, 3, 5, 4):
+        s = (me + k) % 8
+        remote(
+            recv_g.at[x_ch, s], recv_g.at[x_ch, s], h_send.at[1, s], h_recv.at[1, s], me, x_ch
+        ).wait_recv()
+        send(None, lambda s=s: remote(
+            recv_g.at[x_ch, s], recv_g.at[x_ch, s], h_send.at[2, s], h_recv.at[2, s], me, c_ch))
     loads[3].wait()
-    for j in range(3):
+    for j in (0, 2):
         for s in range(8):
             remote(
                 recv_g.at[mates[j], s], recv_g.at[mates[j], s], h_send.at[j, s], h_recv.at[j, s], me, mates[j]

time: 61.5 us -> 58.2 us (0.946)
  Pallas kernels: 59.8 us -> 56 us
    pallas_call x1, Pallas kernels: 59.8 us -> 56 us  [per_device_fused(): pl.pallas_call(fused_kernel, out_shape=jax.ShapeDtypeStruct((rows, width)...]
where the time goes in v4:
time: 58.2 us; the launch traced here: 57.6 us
  Pallas kernels  56 us (96%)
  local copies, waits for them, and re-layouts  1.57 us (3%)
    pallas_call x1, Pallas kernels, per_device_fused(): pl.pallas_call(fused_kernel, out_shape=jax.ShapeDtypeStruct((rows, width)...  56 us
    unnamed x1, local copies, waits for them, and re-layouts  1.57 us

profile of v4, /device:TPU:0, one launch (start us, length us, event | category | flops | bytes accessed | tf_op | source)
XLA Modules:
  0.0 57.6 jit_solution(13971911263935255041)
XLA Ops:
  0.0 56.0 %shard_map.73 = bf16[128,512]{1,0:T(8,128)(2,1)} custom-call(bf16[128,2048]{1,0:T(8,128)(2,1)} %tokens.1, bf16[3,256,512]{2,1,0:T(8,128)(2,1)} %bitcast.2, f32[128,512]{1,0:T(8,128)} %taps_hbm.1, f32[1,512]{1,0:T(1,128)} %bitcast.3, bf16[2048,512]{1,0:T(8,128)(2,1)} %out_weight.1, bf16[2048,1024]{1,0:T(8,128)(2,1)} %constant.4.clone.table_hbm, ...), custom_call_target="tpu_custom_call" | custom-call | tf_op jit(solution)/shard_map/pallas_call | solution.py:476
  56.0 1.6 %copy.9 = bf16[128,512]{1,0:T(8,128)(2,1)} copy(bf16[128,512]{1,0:T(8,128)(2,1)} %shard_map.73) | data formatting | bytes 262144
